TPU v7x, 32 devices: a whole 2x2x4 slice. The times are simulated.
32 devices in a mesh: row: 2 (over x), col: 4 (over z), layer: 4 (over y, core).
Axes of the slice: x: 2, y: 2, z: 4, core: 2. Of those that a mesh axis runs over, the one named last changes fastest.
Arguments:
- a_blocks: bfloat16 [64, 128, 128], P(('row', 'col', 'layer')), may hold values from -0.5 to 0.5
- a_slot: int32 [64], P(('row', 'col', 'layer')), may hold values from 0 to 63, as said below
- b_blocks: bfloat16 [32, 128, 128], P(('row', 'col', 'layer')), may hold values from -6 to 6
- b_slot: int32 [32], P(('row', 'col', 'layer')), may hold values from 0 to 31, as said below
- c_mask: int32 [32, 32], P('row', 'col'), may hold values from 0 to 1, as said below
Outputs:
- product: float32 [4096, 4096], P(('row', 'layer'), 'col')
Inputs may be any that keep to these rules, and one draw needn't show every extreme that they name: `a_slot`: within each row panel r and inner slice l the 8 slots of A are distinct. `b_slot`: within each column panel c and inner slice l the 2 slots of B are distinct. `c_mask`: every block row has exactly 4 ones in each column panel of 8 block columns.
All inputs are finite; a program needn't handle non-finite values.
Results may differ from a plain program's by a relative error of at most 0.0003.
Values may be sent and summed in bfloat16 or wider, within the bound.
No kernel may reach another device: no remote copies, remote signals or barrier semaphores. Data moves between devices by JAX's collectives and lax.ppermute only.
A program may use at most 64 MiB of HBM per device.

v0:
```python
import jax
import jax.numpy as jnp
from jax import lax
from jax.sharding import PartitionSpec as P

MBP = 16
KBL = 4
NBP = 8


def slot_table(slots, count):
    return (slots[:, None] == jnp.arange(count, dtype=jnp.int32)[None, :]).astype(jnp.bfloat16)


def add_blocks(piece):
    table, blocks = piece
    flat = blocks.reshape(blocks.shape[0], blocks.shape[1] * blocks.shape[2])
    return jnp.dot(table.T, flat, preferred_element_type=jnp.float32)


def on_device(a_blocks, a_slot, b_blocks, b_slot, c_mask):
    width = a_blocks.shape[-1]
    a_table = slot_table(a_slot, MBP * KBL)
    b_table = slot_table(b_slot, KBL * NBP)
    a_dense = add_blocks(
        (
            lax.all_gather(a_table, "col", axis=0, tiled=True),
            lax.all_gather(a_blocks, "col", axis=0, tiled=True),
        )
    )
    b_dense = add_blocks(
        (
            lax.all_gather(b_table, "row", axis=0, tiled=True),
            lax.all_gather(b_blocks, "row", axis=0, tiled=True),
        )
    )
    a_matrix = (
        a_dense.astype(jnp.bfloat16)
        .reshape(MBP, KBL, width, width)
        .transpose(0, 2, 1, 3)
        .reshape(MBP * width, KBL * width)
    )
    b_matrix = (
        b_dense.astype(jnp.bfloat16)
        .reshape(KBL, NBP, width, width)
        .transpose(0, 2, 1, 3)
        .reshape(KBL * width, NBP * width)
    )
    partial_value = jnp.dot(a_matrix, b_matrix, preferred_element_type=jnp.float32)
    rows_dev = MBP * width // lax.axis_size("layer")
    first_row = lax.axis_index("layer") * rows_dev
    own_block = (first_row + jnp.arange(rows_dev, dtype=jnp.int32)) // width
    row_pick = (own_block[:, None] == jnp.arange(MBP, dtype=jnp.int32)[None, :]).astype(jnp.float32)
    mask_float = c_mask.astype(jnp.float32)
    summed = lax.psum_scatter(partial_value, "layer", scatter_dimension=0, tiled=True)
    row_mask = jnp.dot(row_pick, mask_float, precision=lax.Precision.HIGHEST)
    return (summed.reshape(rows_dev, NBP, width) * row_mask[:, :, None]).reshape(
        rows_dev, NBP * width
    )


def solution(mesh):
    in_specs = (
        P(("row", "col", "layer"), None, None),
        P(("row", "col", "layer")),
        P(("row", "col", "layer"), None, None),
        P(("row", "col", "layer")),
        P("row", "col"),
    )
    out_specs = P(("row", "layer"), "col")
    return jax.shard_map(
        on_device, mesh=mesh, in_specs=in_specs, out_specs=out_specs, check_vma=False
    )
```

profile of v0, /device:TPU:0, one launch (start us, length us, event | category | flops | bytes accessed | tf_op | source)
XLA Modules:
  0.0 136.6 jit_solution(10987908458039829682)
XLA Ops:
  6.5 0.0 reduce-scatter.2.cloned.1.call-start
  6.5 15.8 %all_gather.13 = bf16[8,128,128]{2,1,0:T(8,128)(2,1)S(1)} all-gather(bf16[2,128,128]{2,1,0:T(8,128)(2,1)} %param.5), channel_id=1, replica_groups=mesh['row'=2,'col'=4,'layer'=4] {'col'}, dimensions={0}, use_global_device_ids=true | all-gather | bytes 327680 | tf_op jit(solution)/shard_map/all_gather | solution.py:28
  22.4 0.7 fusion.16
  23.1 11.4 %all-gather = bf16[4,2,64]{2,1,0:T(2,128)(2,1)S(1)} all-gather(bf16[1,2,64]{2,1,0:T(2,128)(2,1)S(1)} %fusion.16), channel_id=1, replica_groups=mesh['row'=2,'col'=4,'layer'=4] {'col'}, dimensions={0}, use_global_device_ids=true | all-gather | bytes 1280 | tf_op jit(solution)/shard_map/all_gather | solution.py:27
  34.5 0.7 fusion.3
  35.2 0.0 copy-start.1
  35.2 0.6 copy.14
  35.8 0.2 copy-done.1
  36.0 4.6 %all_gather.15 = bf16[2,128,128]{2,1,0:T(8,128)(2,1)S(1)} all-gather(bf16[1,128,128]{2,1,0:T(8,128)(2,1)S(1)} %copy-done.1), channel_id=1, replica_groups=mesh['row'=2,'col'=4,'layer'=4] {'row'}, dimensions={0}, use_global_device_ids=true | all-gather | bytes 98304 | tf_op jit(solution)/shard_map/all_gather | solution.py:34
  41.2 2.9 %copy.9 = bf16[16,4,128,128]{2,0,3,1:T(8,128)(2,1)} copy(bf16[16,4,128,128]{3,2,1,0:T(8,128)(2,1)S(1)} %bitcast.43) | data formatting | bytes 4194304 | tf_op jit(solution)/shard_map/reshape | solution.py:39
  44.1 4.2 %all-gather.1 = bf16[2,1,32]{2,1,0:T(2,128)(2,1)S(1)} all-gather(bf16[1,1,32]{2,1,0:T(2,128)(2,1)S(1)} %fusion.17), channel_id=1, replica_groups=mesh['row'=2,'col'=4,'layer'=4] {'row'}, dimensions={0}, use_global_device_ids=true | all-gather | bytes 192 | tf_op jit(solution)/shard_map/all_gather | solution.py:33
  48.3 0.5 convolution_convert_fusion.1
  48.8 7.2 %fusion = f32[2048,1024]{1,0:T(8,128)} fusion(bf16[64,8,16,128]{3,2,1,0:T(8,128)(2,1)} %bitcast.44, bf16[64,8,8,128]{3,2,1,0:T(8,128)(2,1)S(1)} %bitcast.45), kind=kOutput, calls=%fused_computation.3 | convolution fusion | flops 2147483648 | bytes 11534336 | tf_op jit(solution)/shard_map/dot_general | solution.py:49
  56.1 0.0 copy-start.2
  56.1 0.0 reduce-scatter.2.cloned.1.call-update
  56.1 0.6 copy-done.2
  56.7 0.3 fusion.8
  57.1 69.1 %reduce-scatter.2.cloned.1.call-done = f32[512,1024]{1,0:T(8,128)} async-done(((f32[2048,1024]{1,0:T(8,128)}), f32[512,1024]{1,0:T(8,128)}) %reduce-scatter.2.cloned.1.call-update) | async-done | bytes 2097168 | tf_op jit(solution)/shard_map/reduce_scatter | solution.py:55
  126.2 0.0 copy-start
  126.2 0.6 mul.15
  126.8 1.0 copy-done
  127.8 2.0 %bitcast_multiply_fusion = f32[512,1024]{1,0:T(8,128)} fusion(f32[512,1024]{1,0:T(8,128)S(1)} %copy-done, f32[64,8,8,128]{3,2,1,0:T(8,128)S(1)} %bitcast.42), kind=kLoop, calls=%fused_computation.2 | loop fusion | flops 524288 | bytes 6291456 | tf_op jit(solution)/shard_map/mul | solution.py:57
  (2 shorter events, 0.0 us)
Async XLA Ops:
  6.5 119.6 %reduce-scatter.2.cloned.1.call-start = ((), (), s32[]{:S(2)}) async-start(), calls=%async_computation.1 | async-start | bytes 10485760 | tf_op jit(solution)/shard_map/reduce_scatter | solution.py:55
  35.2 0.8 copy-start.1
  56.1 0.7 copy-start.2
  126.2 1.6 %copy-start = (f32[512,1024]{1,0:T(8,128)S(1)}, f32[512,1024]{1,0:T(8,128)}, u32[]{:S(2)}) copy-start(f32[512,1024]{1,0:T(8,128)} %reduce-scatter.2.cloned.1.call-done) | copy-start | bytes 6291460
Sparse Core Ops, SparseCore 0:
  56.2 69.9 reduce-scatter.1
where the time goes:
time: 137 us
  waiting for transfers between devices  69.1 us (50%)
  blocking collectives  36 us (26%)
  between operations  14.1 us (10%)
  matrix products  8.79 us (6%)
  local copies, waits for them, and re-layouts  5.87 us (4%)
  other arithmetic  2.77 us (2%)
    reduce_scatter x1, waiting for transfers between devices, on_device(): lax.psum_scatter(partial_value, 'layer', scatter_dimension=0, tiled=True)  69.1 us
    all_gather x1, blocking collectives, on_device(): lax.all_gather(a_blocks, 'col', axis=0, tiled=True)  15.8 us
    all_gather x1, blocking collectives, on_device(): lax.all_gather(a_table, 'col', axis=0, tiled=True)  11.4 us
    dot_general x1, matrix products, on_device(): jnp.dot(a_matrix, b_matrix, preferred_element_type=jnp.float32)  7.23 us
    all_gather x1, blocking collectives, on_device(): lax.all_gather(b_blocks, 'row', axis=0, tiled=True)  4.58 us
    all_gather x1, blocking collectives, on_device(): lax.all_gather(b_table, 'row', axis=0, tiled=True)  4.2 us
    reshape x1, local copies, waits for them, and re-layouts, on_device(): a_matrix = a_dense.astype(jnp.bfloat16).reshape(MBP, KBL, width, width).t...  2.89 us
  transfers between devices with their start and end apart: 1, of which 1 were waited for; matrix products, arithmetic and copies ran while one was open for 0% of the time, Pallas kernels for 0%

commit v1 on v0

v1 whole, which is shorter than its diff:
```python
import functools

import jax
import jax.numpy as jnp
from jax import lax
from jax.experimental import pallas as pl
from jax.experimental.pallas import tpu as pltpu
from jax.sharding import PartitionSpec as P

MBP = 16
KBL = 4
NBP = 8
CORES = 2
A_BITS = 17
B_BITS = 5
TILE = 16
ANYWHERE = pl.BlockSpec(memory_space=pl.ANY)
IN_VMEM = pl.BlockSpec(memory_space=pltpu.VMEM)


def blank_kernel(out_ref, blank, sems):
    rows = blank.shape[0]
    blank[...] = jnp.zeros_like(blank)
    copies = []
    for i in range(out_ref.shape[0] // rows):
        copies.append(pltpu.make_async_copy(blank, out_ref.at[i * rows : (i + 1) * rows], sems.at[i]))
        copies[-1].start()
    for copy in copies:
        copy.wait()


def blank_output(rows, width):
    shape = (rows * width, NBP * width)
    return pl.pallas_call(
        blank_kernel,
        out_shape=jax.ShapeDtypeStruct(shape, jnp.float32),
        out_specs=ANYWHERE,
        scratch_shapes=[pltpu.VMEM((width, NBP * width), jnp.float32), pltpu.SemaphoreType.DMA((rows,))],
        cost_estimate=pl.CostEstimate(flops=0, bytes_accessed=2097152, transcendentals=0),
        compiler_params=pltpu.CompilerParams(vmem_limit_bytes=16 * 2**20),
    )()


def multiply_kernel(
    sizes, mask_hbm, blocks, blank_ref, out_ref, mask, slot_rows, slots, row_bits, pairs, acc, sems, out_sems
):
    del blank_ref
    n_layer, n_col, n_row, n_a, n_b = sizes
    width = blocks.shape[-1]
    own_rows = MBP // n_layer
    first_row = lax.axis_index("layer") * own_rows
    a_part = n_a * width + TILE
    b_part = n_b * width + TILE
    a_starts = [0] + [b_part + i * a_part for i in range(1, n_col)]
    b_starts = [a_part] + [n_col * a_part + i * b_part for i in range(1, n_row)]
    stride = n_col * a_part + n_row * b_part
    tile_starts = [at + n_a * width for at in a_starts] + [at + n_b * width for at in b_starts]
    tiles = len(tile_starts)

    mask_copy = pltpu.make_async_copy(mask_hbm, mask, sems.at[0])
    mask_copy.start()
    for q in range(n_layer):
        for i, start in enumerate(tile_starts):
            at = q * stride + start
            tile = blocks[at : at + TILE, :].astype(jnp.float32)
            slot_rows[q * tiles + i, :] = tile[0].astype(jnp.int32)
    slot_copy = pltpu.make_async_copy(slot_rows, slots, sems.at[1])
    slot_copy.start()
    mask_copy.wait()
    for row in range(own_rows):
        bits = mask[0, first_row + row]
        for col in range(1, NBP):
            bits = bits | lax.shift_left(mask[col, first_row + row], col)
        row_bits[row] = bits
    slot_copy.wait()

    def scan(q, count):
        base = q * tiles
        words = []
        for i, start in enumerate(a_starts):
            for t in range(n_a):
                s = slots[base + i, t]
                row = lax.shift_right_logical(s, KBL.bit_length() - 1) - first_row
                near = jnp.clip(row, 0, own_rows - 1)
                bits = jnp.where(row == near, row_bits[near], 0)
                word = lax.shift_left(bits, (s & (KBL - 1)) * NBP)
                at = q * (stride // TILE) + (start + t * width) // TILE
                words.append((word, lax.shift_left(at, A_BITS) + near * NBP))
        for i, start in enumerate(b_starts):
            for t in range(n_b):
                s = slots[base + n_col + i, t]
                at = q * (stride // TILE) + (start + t * width) // TILE
                b_code = lax.shift_left(at, B_BITS) + (s & (NBP - 1))
                for word, a_code in words:
                    pairs[count] = a_code + b_code
                    count = count + (lax.shift_right_logical(word, s) & 1)
        return count

    count = lax.fori_loop(0, n_layer, scan, jnp.int32(0), unroll=n_layer <= 4)
    pairs[count] = 0

    def copy_of(here):
        row = lax.shift_right_logical(here, NBP.bit_length() - 1)
        col = here & (NBP - 1)
        return pltpu.make_async_copy(
            acc.at[here],
            out_ref.at[
                pl.ds(pl.multiple_of(row * width, width), width),
                pl.ds(pl.multiple_of(col * width, width), width),
            ],
            out_sems.at[here],
        )

    def block(at):
        return blocks[pl.ds(pl.multiple_of(at * TILE, TILE), width), :]

    def product(code):
        a_at = lax.shift_right_logical(code, A_BITS)
        b_at = lax.shift_right_logical(code, B_BITS) & (2 ** (A_BITS - B_BITS) - 1)
        return jnp.dot(block(a_at), block(b_at), preferred_element_type=jnp.float32)

    def put(code, value, seen):
        here = code & (2**B_BITS - 1)
        bit = lax.shift_left(jnp.int32(1), here)
        first = (seen & bit) == 0

        @pl.when(first)
        def _():
            acc[here] = value

        @pl.when(jnp.logical_not(first))
        def _():
            copy_of(here).wait()
            acc[here] += value

        copy_of(here).start()
        return seen | bit

    def two_products(n, seen):
        codes = [pairs[2 * n], pairs[2 * n + 1]]
        values = [product(code) for code in codes]
        seen = put(codes[0], values[0], seen)
        return lax.cond(2 * n + 1 < count, lambda: put(codes[1], values[1], seen), lambda: seen)

    seen = lax.fori_loop(0, lax.shift_right_logical(count + 1, 1), two_products, jnp.int32(0))

    def settle(n, left):
        here = pairs[n] & (2**B_BITS - 1)
        bit = lax.shift_left(jnp.int32(1), here)

        @pl.when((left & bit) != 0)
        def _():
            copy_of(here).wait()

        return left & ~bit

    lax.fori_loop(0, count, settle, seen)


def multiply(blocks, mask_t, blank, n_a, n_b):
    n_layer, n_col, n_row = (lax.axis_size(name) for name in ("layer", "col", "row"))
    own_rows = MBP // n_layer
    width = blocks.shape[-1]
    n_pairs = n_layer * n_col * n_a * n_row * n_b
    slot_shape = (n_layer * (n_col + n_row), width)
    return pl.pallas_call(
        functools.partial(multiply_kernel, (n_layer, n_col, n_row, n_a, n_b)),
        out_shape=jax.ShapeDtypeStruct(blank.shape, blank.dtype),
        in_specs=[ANYWHERE, IN_VMEM, ANYWHERE],
        out_specs=ANYWHERE,
        scratch_shapes=[
            pltpu.SMEM(mask_t.shape, jnp.int32),
            pltpu.VMEM(slot_shape, jnp.int32),
            pltpu.SMEM(slot_shape, jnp.int32),
            pltpu.SMEM((own_rows,), jnp.int32),
            pltpu.SMEM((n_pairs + 2,), jnp.int32),
            pltpu.VMEM((own_rows * NBP, width, width), jnp.float32),
            pltpu.SemaphoreType.DMA((2,)),
            pltpu.SemaphoreType.DMA((own_rows * NBP,)),
        ],
        input_output_aliases={2: 0},
        compiler_params=pltpu.CompilerParams(vmem_limit_bytes=48 * 2**20),
    )(mask_t, blocks, blank)


def shift(value, axis, step):
    size = lax.axis_size(axis)
    return lax.ppermute(value, axis, [(i, (i + step) % size) for i in range(size)])


def to_other_core(value):
    size = lax.axis_size("layer")
    return lax.ppermute(value, "layer", [(i, i ^ 1) for i in range(size)])


def pack_kernel(a_hbm, slot_hbm, b_hbm, out, slots, sems):
    a_rows = a_hbm.shape[0]
    moves = ((slot_hbm, slots), (a_hbm, out.at[:a_rows]), (b_hbm, out.at[a_rows + TILE :]))
    copies = [pltpu.make_async_copy(x, y, sems.at[i]) for i, (x, y) in enumerate(moves)]
    for copy in copies:
        copy.start()
    lane = lax.broadcasted_iota(jnp.int32, (TILE, out.shape[-1]), 1)
    copies[0].wait()
    tile = jnp.zeros(lane.shape, jnp.int32)
    for i in range(slots.shape[0]):
        tile = jnp.where(lane == i, slots[i], tile)
    out[a_rows : a_rows + TILE, :] = tile.astype(jnp.float32).astype(out.dtype)
    copies[1].wait()
    copies[2].wait()


def pack(a_blocks, a_slot, b_blocks):
    width = a_blocks.shape[-1]
    args = [a_blocks.reshape(-1, width), a_slot, b_blocks.reshape(-1, width)]
    a, a_slot, b = [pltpu.with_memory_space_constraint(x, pltpu.HBM) for x in args]
    return pl.pallas_call(
        pack_kernel,
        out_shape=jax.ShapeDtypeStruct((a.shape[0] + TILE + b.shape[0], width), a.dtype),
        in_specs=[pl.BlockSpec(memory_space=pltpu.HBM)] * 3,
        out_specs=IN_VMEM,
        scratch_shapes=[pltpu.SMEM(a_slot.shape, jnp.int32), pltpu.SemaphoreType.DMA((3,))],
        compiler_params=pltpu.CompilerParams(vmem_limit_bytes=16 * 2**20),
    )(a, a_slot, b)


def slot_tile(slots, width, dtype):
    row = slots.astype(dtype)[None, :]
    return jnp.pad(row, ((0, TILE - 1), (0, width - slots.shape[0])))


def joined(parts):
    return jnp.concatenate(parts, axis=0) if len(parts) > 1 else parts[0]


def split(value, likes):
    parts, at = [], 0
    for like in likes:
        parts.append(lax.slice_in_dim(value, at, at + like.shape[0], axis=0))
        at += like.shape[0]
    return parts


def on_device(a_blocks, a_slot, b_blocks, b_slot, c_mask):
    n_layer, n_col, n_row = (lax.axis_size(name) for name in ("layer", "col", "row"))
    n_a, n_b = a_blocks.shape[0], b_blocks.shape[0]
    far = range(CORES, n_layer, CORES)
    middle = n_col // 2
    sides = [s for s in range(1, n_col) if s != middle]

    width = a_blocks.shape[-1]
    a_rows = n_a * width + TILE
    packed = pack(a_blocks, a_slot, b_blocks)
    a_own = packed[:a_rows]
    own = joined([packed, slot_tile(b_slot, width, a_own.dtype)])

    a_sides = [shift(a_own, "col", s) for s in sides]
    a_middle = shift(a_own, "col", middle)
    blank = blank_output(MBP // n_layer, width)
    a_sides, blank = lax.optimization_barrier((a_sides, blank))
    own_far = [shift(own, "layer", s) for s in far]
    side_pair = joined(a_sides)
    sides_far = [shift(side_pair, "layer", s) for s in far]
    late = joined([a_middle, own_far[0][-TILE:]])
    middle_far = [shift(late, "layer", s)[:a_rows] for s in far]
    b_line = joined([p[a_rows:] for p in [own] + own_far])
    b_across = [shift(b_line, "row", s) for s in range(1, n_row)]

    b_rows = own.shape[0] - a_rows
    near = {(j, 0, 0): p for j, p in enumerate([own] + own_far)}
    near |= {(0, 1, 0): side_pair, (0, 1, 1): a_middle}
    for i, p in enumerate(b_across):
        near |= {(j, 2, i): p[j * b_rows : (j + 1) * b_rows] for j in range(1 + len(far))}
    distant = {}
    for j in range(len(far)):
        distant |= {(1 + j, 1, 0): sides_far[j], (1 + j, 1, 1): middle_far[j]}
    pools = [near, distant]
    here = [lax.optimization_barrier(joined(list(pool.values()))) for pool in pools]
    other = [to_other_core(p) for p in here]

    def in_order(wholes):
        parts = {}
        for pool, whole in zip(pools, wholes):
            parts |= dict(zip(pool, split(whole, pool.values())))
        return [parts[key] for key in sorted(parts)]

    blocks = joined(in_order(here) + in_order(other))
    return multiply(blocks, c_mask.T, blank, n_a, n_b)


def solution(mesh):
    in_specs = (
        P(("row", "col", "layer"), None, None),
        P(("row", "col", "layer")),
        P(("row", "col", "layer"), None, None),
        P(("row", "col", "layer")),
        P("row", "col"),
    )
    out_specs = P(("row", "layer"), "col")
    return jax.shard_map(
        on_device, mesh=mesh, in_specs=in_specs, out_specs=out_specs, check_vma=False
    )
```

time: 137 us -> 23.5 us (0.17)
  waiting for transfers between devices: 69.1 us -> 4.94 us
  blocking collectives: 36 us -> 0 us
  between operations: 14.1 us -> 0.91 us
  starting transfers between devices: 0.01 us -> 12.3 us
  matrix products: 8.79 us -> 0 us
  local copies, waits for them, and re-layouts: 5.87 us -> 0.33 us
  Pallas kernels: 0 us -> 5.05 us
  other arithmetic: 2.77 us -> 0.06 us
    reduce_scatter x1 -> x0, waiting for transfers between devices: 69.1 us -> none  [on_device(): lax.psum_scatter(partial_value, 'layer', scatter_dimension=0, tiled=True)]
    all_gather x4 -> x0, blocking collectives: 36 us -> none  [the longest x1 15.8 us: on_device(): lax.all_gather(a_blocks, 'col', axis=0, tiled=True)]
    ppermute x0 -> x9, starting transfers between devices: none -> 12.3 us  [the longest x7 12.2 us: shift(): lax.ppermute(value, axis, [(i, (i + step) % size) for i in range(size)])]
    dot_general x4 -> x0, matrix products: 8.79 us -> none  [the longest x1 7.23 us: on_device(): jnp.dot(a_matrix, b_matrix, preferred_element_type=jnp.float32)]
    pallas_call x0 -> x3, Pallas kernels: none -> 5.05 us  [the longest x1 2.8 us: multiply(): pl.pallas_call(functools.partial(multiply_kernel, (n_layer, n_col, n_row,...]
    ppermute x0 -> x9, waiting for transfers between devices: none -> 4.94 us  [the longest x7 3.64 us: shift(): lax.ppermute(value, axis, [(i, (i + step) % size) for i in range(size)])]
    reshape x1 -> x0, local copies, waits for them, and re-layouts: 2.89 us -> none  [on_device(): a_matrix = a_dense.astype(jnp.bfloat16).reshape(MBP, KBL, width, width).t...]
    unnamed x7 -> x17, local copies, waits for them, and re-layouts: 2.38 us -> 0.28 us
  transfers between devices with their start and end apart: 1 -> 9, of which waited for: 1 -> 4; matrix products, arithmetic and copies ran while one was open for 0% -> 1% of each run, Pallas kernels for 0% -> 6%
where the time goes in v1:
time: 23.5 us; the launch traced here: 23.6 us
  starting transfers between devices  12.3 us (52%)
  Pallas kernels  5.05 us (21%)
  waiting for transfers between devices  4.94 us (21%)
  between operations  0.91 us (4%)
  local copies, waits for them, and re-layouts  0.33 us (1%)
    ppermute x7, starting transfers between devices, shift(): lax.ppermute(value, axis, [(i, (i + step) % size) for i in range(size)])  12.2 us
    ppermute x7, waiting for transfers between devices, shift(): lax.ppermute(value, axis, [(i, (i + step) % size) for i in range(size)])  3.64 us
    pallas_call x1, Pallas kernels, multiply(): pl.pallas_call(functools.partial(multiply_kernel, (n_layer, n_col, n_row,...  2.8 us
    pallas_call x1, Pallas kernels, blank_output(): pl.pallas_call(blank_kernel, out_shape=jax.ShapeDtypeStruct(shape, jnp.fl...  1.38 us
    ppermute x2, waiting for transfers between devices, to_other_core(): return lax.ppermute(value, 'layer', [(i, i ^ 1) for i in range(size)])  1.29 us
    pallas_call x1, Pallas kernels, pack(): pl.pallas_call(pack_kernel, out_shape=jax.ShapeDtypeStruct((a.shape[0] +...  0.87 us
  transfers between devices with their start and end apart: 9, of which 4 were waited for; matrix products, arithmetic and copies ran while one was open for 1% of the time, Pallas kernels for 6%

profile of v1, /device:TPU:0, one launch (start us, length us, event | category | flops | bytes accessed | tf_op | source)
XLA Modules:
  0.0 23.6 jit_solution(14767690355801111764)
XLA Ops:
  0.0 0.9 %shard_map.55 = bf16[400,128]{1,0:T(8,128)(2,1)S(1)} custom-call(bf16[256,128]{1,0:T(8,128)(2,1)} %bitcast.5, s32[2]{0:T(128)} %slot_hbm.1, bf16[128,128]{1,0:T(8,128)(2,1)} %bitcast.6), custom_call_target="tpu_custom_call" | custom-call | tf_op jit(solution)/shard_map/pallas_call | solution.py:216
  0.9 3.1 %collective-permute-start.1 = (bf16[272,128]{1,0:T(8,128)(2,1)S(1)}, bf16[272,128]{1,0:T(8,128)(2,1)S(1)}, u32[]{:S(2)}, u32[]{:S(2)}) collective-permute-start(bf16[272,128]{1,0:T(8,128)(2,1)S(1)} %slice.67), channel_id=1, source_target_pairs={{0,4},{4,8},{8,12},{12,0},{1,5},{5,9},{9,13},{13,1},{2,6},{6,10},{... | collective-permute-start | bytes 208904 | tf_op jit(solution)/shard_map/ppermute | solution.py:188
  4.0 2.1 %collective-permute-start.2 = (bf16[272,128]{1,0:T(8,128)(2,1)S(1)}, bf16[272,128]{1,0:T(8,128)(2,1)S(1)}, u32[]{:S(2)}, u32[]{:S(2)}) collective-permute-start(bf16[272,128]{1,0:T(8,128)(2,1)S(1)} %slice.67), channel_id=1, source_target_pairs={{0,12},{4,0},{8,4},{12,8},{1,13},{5,1},{9,5},{13,9},{2,14},{6,2},{... | collective-permute-start | bytes 208904 | tf_op jit(solution)/shard_map/ppermute | solution.py:188
  6.1 0.9 %collective-permute-start.3 = (bf16[272,128]{1,0:T(8,128)(2,1)S(1)}, bf16[272,128]{1,0:T(8,128)(2,1)S(1)}, u32[]{:S(2)}, u32[]{:S(2)}) collective-permute-start(bf16[272,128]{1,0:T(8,128)(2,1)S(1)} %slice.67), channel_id=1, source_target_pairs={{0,8},{4,12},{8,0},{12,4},{1,9},{5,13},{9,1},{13,5},{2,10},{6,14},... | collective-permute-start | bytes 208904 | tf_op jit(solution)/shard_map/ppermute | solution.py:188
  7.7 1.6 %collective-permute-start = (bf16[416,128]{1,0:T(8,128)(2,1)S(1)}, bf16[416,128]{1,0:T(8,128)(2,1)S(1)}, u32[]{:S(2)}, u32[]{:S(2)}) collective-permute-start(bf16[416,128]{1,0:T(8,128)(2,1)S(1)} %pad_maximum_fusion.1), channel_id=1, source_target_pairs={{0,2},{1,3},{2,0},{3,1},{4,6},{5,7},{6,4},{7,5},{8,10},{9,11},{10,... | collective-permute-start | bytes 319496 | tf_op jit(solution)/shard_map/ppermute | solution.py:188
  9.3 1.4 %shard_map.56.blank_ref = f32[512,1024]{1,0:T(8,128)} custom-call(), custom_call_target="tpu_custom_call" | custom-call | bytes 2097152 | tf_op jit(solution)/shard_map/pallas_call | solution.py:34
  10.7 0.0 collective-permute-done.1
  10.7 0.0 collective-permute-done.2
  10.8 0.6 %collective-permute-start.5 = (bf16[544,128]{1,0:T(8,128)(2,1)S(1)}, bf16[544,128]{1,0:T(8,128)(2,1)S(1)}, u32[]{:S(2)}, u32[]{:S(2)}) collective-permute-start(bf16[544,128]{1,0:T(8,128)(2,1)S(1)} %pad_maximum_fusion.2), channel_id=1, source_target_pairs={{0,2},{1,3},{2,0},{3,1},{4,6},{5,7},{6,4},{7,5},{8,10},{9,11},{10,... | collective-permute-start | bytes 417800 | tf_op jit(solution)/shard_map/ppermute | solution.py:188
  11.3 1.5 %collective-permute-done = bf16[416,128]{1,0:T(8,128)(2,1)S(1)} collective-permute-done((bf16[416,128]{1,0:T(8,128)(2,1)S(1)}, bf16[416,128]{1,0:T(8,128)(2,1)S(1)}, u32[]{:S(2)}, u32[]{:S(2)}) %collective-permute-start) | collective-permute-done | bytes 106528 | tf_op jit(solution)/shard_map/ppermute | solution.py:188
  12.9 1.6 %collective-permute-start.4 = (bf16[288,128]{1,0:T(8,128)(2,1)S(1)}, bf16[288,128]{1,0:T(8,128)(2,1)S(1)}, u32[]{:S(2)}, u32[]{:S(2)}) collective-permute-start(bf16[288,128]{1,0:T(8,128)(2,1)S(1)} %pad_maximum_fusion.3), channel_id=1, source_target_pairs={{0,16},{16,0},{1,17},{17,1},{2,18},{18,2},{3,19},{19,3},{4,20},{20... | collective-permute-start | bytes 221192 | tf_op jit(solution)/shard_map/ppermute | solution.py:188
  14.5 0.0 collective-permute-done.3
  14.5 2.4 %collective-permute-start.6 = (bf16[288,128]{1,0:T(8,128)(2,1)S(1)}, bf16[288,128]{1,0:T(8,128)(2,1)S(1)}, u32[]{:S(2)}, u32[]{:S(2)}) collective-permute-start(bf16[288,128]{1,0:T(8,128)(2,1)S(1)} %pad_maximum_fusion.4), channel_id=1, source_target_pairs={{0,2},{1,3},{2,0},{3,1},{4,6},{5,7},{6,4},{7,5},{8,10},{9,11},{10,... | collective-permute-start | bytes 221192 | tf_op jit(solution)/shard_map/ppermute | solution.py:188
  16.9 0.4 %collective-permute-done.4 = bf16[288,128]{1,0:T(8,128)(2,1)S(1)} collective-permute-done((bf16[288,128]{1,0:T(8,128)(2,1)S(1)}, bf16[288,128]{1,0:T(8,128)(2,1)S(1)}, u32[]{:S(2)}, u32[]{:S(2)}) %collective-permute-start.4) | collective-permute-done | bytes 73760 | tf_op jit(solution)/shard_map/ppermute | solution.py:188
  17.3 0.1 collective-permute-start.7
  17.5 0.0 copy-start
  17.5 1.7 %collective-permute-done.6 = bf16[288,128]{1,0:T(8,128)(2,1)S(1)} collective-permute-done((bf16[288,128]{1,0:T(8,128)(2,1)S(1)}, bf16[288,128]{1,0:T(8,128)(2,1)S(1)}, u32[]{:S(2)}, u32[]{:S(2)}) %collective-permute-start.6) | collective-permute-done | bytes 73760 | tf_op jit(solution)/shard_map/ppermute | solution.py:188
  19.2 0.0 collective-permute-done.5
  19.2 0.1 collective-permute-start.8
  19.4 0.0 collective-permute-done.7
  19.5 1.3 %collective-permute-done.8 = bf16[816,128]{1,0:T(8,128)(2,1)S(1)} collective-permute-done((bf16[816,128]{1,0:T(8,128)(2,1)S(1)}, bf16[816,128]{1,0:T(8,128)(2,1)S(1)}, u32[]{:S(2)}, u32[]{:S(2)}) %collective-permute-start.8) | collective-permute-done | bytes 208928 | tf_op jit(solution)/shard_map/ppermute | solution.py:193
  20.8 0.0 copy-done
  20.8 2.8 %shard_map.57 = f32[512,1024]{1,0:T(8,128)} custom-call(s32[8,16]{1,0:T(8,128)S(1)} %bitcast.4, bf16[5504,128]{1,0:T(8,128)(2,1)S(1)} %slice_dynamic-update-slice_fusion.6.blocks, f32[512,1024]{1,0:T(8,128)} %shard_map.56.blank_ref), custom_call_target="tpu_custom_call", output_to_operand_aliasing={{}: (2, {})} | custom-call | tf_op jit(solution)/shard_map/pallas_call | solution.py:166
  (28 shorter events, 0.4 us)
Async XLA Ops:
  0.9 9.8 %collective-permute-start.1 = (bf16[272,128]{1,0:T(8,128)(2,1)S(1)}, bf16[272,128]{1,0:T(8,128)(2,1)S(1)}, u32[]{:S(2)}, u32[]{:S(2)}) collective-permute-start(bf16[272,128]{1,0:T(8,128)(2,1)S(1)} %slice.67), channel_id=1, source_target_pairs={{0,4},{4,8},{8,12},{12,0},{1,5},{5,9},{9,13},{13,1},{2,6},{6,10},{... | collective-permute-start | bytes 208904 | tf_op jit(solution)/shard_map/ppermute | solution.py:188
  4.0 6.8 %collective-permute-start.2 = (bf16[272,128]{1,0:T(8,128)(2,1)S(1)}, bf16[272,128]{1,0:T(8,128)(2,1)S(1)}, u32[]{:S(2)}, u32[]{:S(2)}) collective-permute-start(bf16[272,128]{1,0:T(8,128)(2,1)S(1)} %slice.67), channel_id=1, source_target_pairs={{0,12},{4,0},{8,4},{12,8},{1,13},{5,1},{9,5},{13,9},{2,14},{6,2},{... | collective-permute-start | bytes 208904 | tf_op jit(solution)/shard_map/ppermute | solution.py:188
  6.1 8.4 %collective-permute-start.3 = (bf16[272,128]{1,0:T(8,128)(2,1)S(1)}, bf16[272,128]{1,0:T(8,128)(2,1)S(1)}, u32[]{:S(2)}, u32[]{:S(2)}) collective-permute-start(bf16[272,128]{1,0:T(8,128)(2,1)S(1)} %slice.67), channel_id=1, source_target_pairs={{0,8},{4,12},{8,0},{12,4},{1,9},{5,13},{9,1},{13,5},{2,10},{6,14},... | collective-permute-start | bytes 208904 | tf_op jit(solution)/shard_map/ppermute | solution.py:188
  7.7 5.1 %collective-permute-start = (bf16[416,128]{1,0:T(8,128)(2,1)S(1)}, bf16[416,128]{1,0:T(8,128)(2,1)S(1)}, u32[]{:S(2)}, u32[]{:S(2)}) collective-permute-start(bf16[416,128]{1,0:T(8,128)(2,1)S(1)} %pad_maximum_fusion.1), channel_id=1, source_target_pairs={{0,2},{1,3},{2,0},{3,1},{4,6},{5,7},{6,4},{7,5},{8,10},{9,11},{10,... | collective-permute-start | bytes 319496 | tf_op jit(solution)/shard_map/ppermute | solution.py:188
  10.8 8.4 %collective-permute-start.5 = (bf16[544,128]{1,0:T(8,128)(2,1)S(1)}, bf16[544,128]{1,0:T(8,128)(2,1)S(1)}, u32[]{:S(2)}, u32[]{:S(2)}) collective-permute-start(bf16[544,128]{1,0:T(8,128)(2,1)S(1)} %pad_maximum_fusion.2), channel_id=1, source_target_pairs={{0,2},{1,3},{2,0},{3,1},{4,6},{5,7},{6,4},{7,5},{8,10},{9,11},{10,... | collective-permute-start | bytes 417800 | tf_op jit(solution)/shard_map/ppermute | solution.py:188
  12.9 4.4 %collective-permute-start.4 = (bf16[288,128]{1,0:T(8,128)(2,1)S(1)}, bf16[288,128]{1,0:T(8,128)(2,1)S(1)}, u32[]{:S(2)}, u32[]{:S(2)}) collective-permute-start(bf16[288,128]{1,0:T(8,128)(2,1)S(1)} %pad_maximum_fusion.3), channel_id=1, source_target_pairs={{0,16},{16,0},{1,17},{17,1},{2,18},{18,2},{3,19},{19,3},{4,20},{20... | collective-permute-start | bytes 221192 | tf_op jit(solution)/shard_map/ppermute | solution.py:188
  14.5 4.7 %collective-permute-start.6 = (bf16[288,128]{1,0:T(8,128)(2,1)S(1)}, bf16[288,128]{1,0:T(8,128)(2,1)S(1)}, u32[]{:S(2)}, u32[]{:S(2)}) collective-permute-start(bf16[288,128]{1,0:T(8,128)(2,1)S(1)} %pad_maximum_fusion.4), channel_id=1, source_target_pairs={{0,2},{1,3},{2,0},{3,1},{4,6},{5,7},{6,4},{7,5},{8,10},{9,11},{10,... | collective-permute-start | bytes 221192 | tf_op jit(solution)/shard_map/ppermute | solution.py:188
  17.3 2.0 %collective-permute-start.7 = (bf16[1936,128]{1,0:T(8,128)(2,1)S(1)}, bf16[1936,128]{1,0:T(8,128)(2,1)S(1)}, u32[]{:S(2)}, u32[]{:S(2)}) collective-permute-start(bf16[1936,128]{1,0:T(8,128)(2,1)S(1)} %constant_dynamic-update-slice_fusion), channel_id=1, source_target_pairs={{0,1},{1,0},{2,3},{3,2},{4,5},{5,4},{6,7},{7,6},{8,9},{9,8},{10,11... | collective-permute-start | bytes 1486856 | tf_op jit(solution)/shard_map/ppermute | solution.py:193
  17.5 3.3 %copy-start = (s32[16,8]{0,1:T(8,128)S(1)}, s32[16,8]{0,1:T(8,128)}, u32[]{:S(2)}) copy-start(s32[16,8]{0,1:T(8,128)} %param.9) | copy-start | bytes 1540
  19.2 1.5 %collective-permute-start.8 = (bf16[816,128]{1,0:T(8,128)(2,1)S(1)}, bf16[816,128]{1,0:T(8,128)(2,1)S(1)}, u32[]{:S(2)}, u32[]{:S(2)}) collective-permute-start(bf16[816,128]{1,0:T(8,128)(2,1)S(1)} %pad_maximum_fusion), channel_id=1, source_target_pairs={{0,1},{1,0},{2,3},{3,2},{4,5},{5,4},{6,7},{7,6},{8,9},{9,8},{10,11... | collective-permute-start | bytes 626696 | tf_op jit(solution)/shard_map/ppermute | solution.py:193

commit v2 on v1

--- a/solution.py
+++ b/solution.py
@@ -14,6 +14,7 @@
 A_BITS = 17
 B_BITS = 5
 TILE = 16
+LANES = 8
 ANYWHERE = pl.BlockSpec(memory_space=pl.ANY)
 IN_VMEM = pl.BlockSpec(memory_space=pltpu.VMEM)
 
@@ -55,15 +56,16 @@
     b_starts = [a_part] + [n_col * a_part + i * b_part for i in range(1, n_row)]
     stride = n_col * a_part + n_row * b_part
     tile_starts = [at + n_a * width for at in a_starts] + [at + n_b * width for at in b_starts]
-    tiles = len(tile_starts)
 
     mask_copy = pltpu.make_async_copy(mask_hbm, mask, sems.at[0])
     mask_copy.start()
     for q in range(n_layer):
+        row = jnp.zeros((TILE // 2, width), jnp.float32)
         for i, start in enumerate(tile_starts):
             at = q * stride + start
-            tile = blocks[at : at + TILE, :].astype(jnp.float32)
-            slot_rows[q * tiles + i, :] = tile[0].astype(jnp.int32)
+            tile = blocks[at : at + TILE, :].astype(jnp.float32)[: TILE // 2]
+            row = row + (pltpu.roll(tile, i * LANES, 1) if i else tile)
+        slot_rows[q, :] = row[0].astype(jnp.int32)
     slot_copy = pltpu.make_async_copy(slot_rows, slots, sems.at[1])
     slot_copy.start()
     mask_copy.wait()
@@ -75,11 +77,10 @@
     slot_copy.wait()
 
     def scan(q, count):
-        base = q * tiles
         words = []
         for i, start in enumerate(a_starts):
             for t in range(n_a):
-                s = slots[base + i, t]
+                s = slots[q, i * LANES + t]
                 row = lax.shift_right_logical(s, KBL.bit_length() - 1) - first_row
                 near = jnp.clip(row, 0, own_rows - 1)
                 bits = jnp.where(row == near, row_bits[near], 0)
@@ -88,7 +89,7 @@
                 words.append((word, lax.shift_left(at, A_BITS) + near * NBP))
         for i, start in enumerate(b_starts):
             for t in range(n_b):
-                s = slots[base + n_col + i, t]
+                s = slots[q, (n_col + i) * LANES + t]
                 at = q * (stride // TILE) + (start + t * width) // TILE
                 b_code = lax.shift_left(at, B_BITS) + (s & (NBP - 1))
                 for word, a_code in words:
@@ -162,7 +163,7 @@
     own_rows = MBP // n_layer
     width = blocks.shape[-1]
     n_pairs = n_layer * n_col * n_a * n_row * n_b
-    slot_shape = (n_layer * (n_col + n_row), width)
+    slot_shape = (n_layer, width)
     return pl.pallas_call(
         functools.partial(multiply_kernel, (n_layer, n_col, n_row, n_a, n_b)),
         out_shape=jax.ShapeDtypeStruct(blank.shape, blank.dtype),
@@ -244,35 +245,33 @@
     n_layer, n_col, n_row = (lax.axis_size(name) for name in ("layer", "col", "row"))
     n_a, n_b = a_blocks.shape[0], b_blocks.shape[0]
     far = range(CORES, n_layer, CORES)
-    middle = n_col // 2
-    sides = [s for s in range(1, n_col) if s != middle]
-
     width = a_blocks.shape[-1]
     a_rows = n_a * width + TILE
     packed = pack(a_blocks, a_slot, b_blocks)
-    a_own = packed[:a_rows]
-    own = joined([packed, slot_tile(b_slot, width, a_own.dtype)])
-
-    a_sides = [shift(a_own, "col", s) for s in sides]
-    a_middle = shift(a_own, "col", middle)
+    own = joined([packed, slot_tile(b_slot, width, packed.dtype)])
+    own = lax.optimization_barrier(own)
+
+    steps = sorted(range(1, n_col), key=lambda s: s != n_col // 2)
+    a_sides = [shift(packed[:a_rows], "col", s) for s in steps[:-1]]
+    a_last = shift(own[:a_rows], "col", steps[-1])
     blank = blank_output(MBP // n_layer, width)
     a_sides, blank = lax.optimization_barrier((a_sides, blank))
     own_far = [shift(own, "layer", s) for s in far]
     side_pair = joined(a_sides)
     sides_far = [shift(side_pair, "layer", s) for s in far]
-    late = joined([a_middle, own_far[0][-TILE:]])
-    middle_far = [shift(late, "layer", s)[:a_rows] for s in far]
+    late = joined([a_last, own_far[0][-TILE:]])
+    last_far = [shift(late, "layer", s)[:a_rows] for s in far]
     b_line = joined([p[a_rows:] for p in [own] + own_far])
     b_across = [shift(b_line, "row", s) for s in range(1, n_row)]
 
     b_rows = own.shape[0] - a_rows
     near = {(j, 0, 0): p for j, p in enumerate([own] + own_far)}
-    near |= {(0, 1, 0): side_pair, (0, 1, 1): a_middle}
+    near |= {(0, 1, 0): side_pair, (0, 1, 1): a_last}
     for i, p in enumerate(b_across):
         near |= {(j, 2, i): p[j * b_rows : (j + 1) * b_rows] for j in range(1 + len(far))}
     distant = {}
     for j in range(len(far)):
-        distant |= {(1 + j, 1, 0): sides_far[j], (1 + j, 1, 1): middle_far[j]}
+        distant |= {(1 + j, 1, 0): sides_far[j], (1 + j, 1, 1): last_far[j]}
     pools = [near, distant]
     here = [lax.optimization_barrier(joined(list(pool.values()))) for pool in pools]
     other = [to_other_core(p) for p in here]

time: 23.5 us -> 23.1 us (0.983)
  starting transfers between devices: 12.3 us -> 13.4 us
  waiting for transfers between devices: 4.94 us -> 3.95 us
  Pallas kernels: 5.05 us -> 4.46 us
    ppermute x7, starting transfers between devices: 12.2 us -> 13.2 us  [shift(): lax.ppermute(value, axis, [(i, (i + step) % size) for i in range(size)])]
    ppermute x7, waiting for transfers between devices: 3.64 us -> 2.64 us  [shift(): lax.ppermute(value, axis, [(i, (i + step) % size) for i in range(size)])]
    pallas_call x1, Pallas kernels: 2.8 us -> 2.21 us  [multiply(): pl.pallas_call(functools.partial(multiply_kernel, (n_layer, n_col, n_row,...]
where the time goes in v2:
time: 23.1 us; the launch traced here: 23 us
  starting transfers between devices  13.4 us (58%)
  Pallas kernels  4.46 us (19%)
  waiting for transfers between devices  3.95 us (17%)
  between operations  0.89 us (4%)
  local copies, waits for them, and re-layouts  0.32 us (1%)
    ppermute x7, starting transfers between devices, shift(): lax.ppermute(value, axis, [(i, (i + step) % size) for i in range(size)])  13.2 us
    ppermute x7, waiting for transfers between devices, shift(): lax.ppermute(value, axis, [(i, (i + step) % size) for i in range(size)])  2.64 us
    pallas_call x1, Pallas kernels, multiply(): pl.pallas_call(functools.partial(multiply_kernel, (n_layer, n_col, n_row,...  2.21 us
    pallas_call x1, Pallas kernels, blank_output(): pl.pallas_call(blank_kernel, out_shape=jax.ShapeDtypeStruct(shape, jnp.fl...  1.38 us
    ppermute x2, waiting for transfers between devices, to_other_core(): return lax.ppermute(value, 'layer', [(i, i ^ 1) for i in range(size)])  1.31 us
    pallas_call x1, Pallas kernels, pack(): pl.pallas_call(pack_kernel, out_shape=jax.ShapeDtypeStruct((a.shape[0] +...  0.87 us
  transfers between devices with their start and end apart: 9, of which 4 were waited for; matrix products, arithmetic and copies ran while one was open for 1% of the time, Pallas kernels for 6%

profile of v2, /device:TPU:0, one launch (start us, length us, event | category | flops | bytes accessed | tf_op | source)
XLA Modules:
  0.0 23.0 jit_solution(187554929321993918)
XLA Ops:
  0.0 0.9 %shard_map.55 = bf16[400,128]{1,0:T(8,128)(2,1)S(1)} custom-call(bf16[256,128]{1,0:T(8,128)(2,1)} %bitcast.5, s32[2]{0:T(128)} %slot_hbm.1, bf16[128,128]{1,0:T(8,128)(2,1)} %bitcast.6), custom_call_target="tpu_custom_call" | custom-call | tf_op jit(solution)/shard_map/pallas_call | solution.py:217
  0.9 4.1 %collective-permute-start.1 = (bf16[272,128]{1,0:T(8,128)(2,1)S(1)}, bf16[272,128]{1,0:T(8,128)(2,1)S(1)}, u32[]{:S(2)}, u32[]{:S(2)}) collective-permute-start(bf16[272,128]{1,0:T(8,128)(2,1)S(1)} %slice.72), channel_id=1, source_target_pairs={{0,8},{4,12},{8,0},{12,4},{1,9},{5,13},{9,1},{13,5},{2,10},{6,14},... | collective-permute-start | bytes 208904 | tf_op jit(solution)/shard_map/ppermute | solution.py:189
  5.0 1.6 %collective-permute-start.2 = (bf16[272,128]{1,0:T(8,128)(2,1)S(1)}, bf16[272,128]{1,0:T(8,128)(2,1)S(1)}, u32[]{:S(2)}, u32[]{:S(2)}) collective-permute-start(bf16[272,128]{1,0:T(8,128)(2,1)S(1)} %slice.72), channel_id=1, source_target_pairs={{0,4},{4,8},{8,12},{12,0},{1,5},{5,9},{9,13},{13,1},{2,6},{6,10},{... | collective-permute-start | bytes 208904 | tf_op jit(solution)/shard_map/ppermute | solution.py:189
  7.2 1.6 %collective-permute-start = (bf16[416,128]{1,0:T(8,128)(2,1)S(1)}, bf16[416,128]{1,0:T(8,128)(2,1)S(1)}, u32[]{:S(2)}, u32[]{:S(2)}) collective-permute-start(bf16[416,128]{1,0:T(8,128)(2,1)S(1)} %fusion.1), channel_id=1, source_target_pairs={{0,2},{1,3},{2,0},{3,1},{4,6},{5,7},{6,4},{7,5},{8,10},{9,11},{10,... | collective-permute-start | bytes 319496 | tf_op jit(solution)/shard_map/ppermute | solution.py:189
  8.8 2.2 %collective-permute-start.3 = (bf16[272,128]{1,0:T(8,128)(2,1)S(1)}, bf16[272,128]{1,0:T(8,128)(2,1)S(1)}, u32[]{:S(2)}, u32[]{:S(2)}) collective-permute-start(bf16[272,128]{1,0:T(8,128)(2,1)S(1)} %slice.73), channel_id=1, source_target_pairs={{0,12},{4,0},{8,4},{12,8},{1,13},{5,1},{9,5},{13,9},{2,14},{6,2},{... | collective-permute-start | bytes 208904 | tf_op jit(solution)/shard_map/ppermute | solution.py:189
  11.1 1.4 %shard_map.56.blank_ref = f32[512,1024]{1,0:T(8,128)} custom-call(), custom_call_target="tpu_custom_call" | custom-call | bytes 2097152 | tf_op jit(solution)/shard_map/pallas_call | solution.py:35
  12.5 0.0 collective-permute-done.1
  12.5 0.0 collective-permute-done.2
  12.5 0.6 %collective-permute-start.5 = (bf16[544,128]{1,0:T(8,128)(2,1)S(1)}, bf16[544,128]{1,0:T(8,128)(2,1)S(1)}, u32[]{:S(2)}, u32[]{:S(2)}) collective-permute-start(bf16[544,128]{1,0:T(8,128)(2,1)S(1)} %pad_maximum_fusion.1), channel_id=1, source_target_pairs={{0,2},{1,3},{2,0},{3,1},{4,6},{5,7},{6,4},{7,5},{8,10},{9,11},{10,... | collective-permute-start | bytes 417800 | tf_op jit(solution)/shard_map/ppermute | solution.py:189
  13.1 0.0 collective-permute-done
  13.2 1.6 %collective-permute-start.4 = (bf16[288,128]{1,0:T(8,128)(2,1)S(1)}, bf16[288,128]{1,0:T(8,128)(2,1)S(1)}, u32[]{:S(2)}, u32[]{:S(2)}) collective-permute-start(bf16[288,128]{1,0:T(8,128)(2,1)S(1)} %pad_maximum_fusion.2), channel_id=1, source_target_pairs={{0,16},{16,0},{1,17},{17,1},{2,18},{18,2},{3,19},{19,3},{4,20},{20... | collective-permute-start | bytes 221192 | tf_op jit(solution)/shard_map/ppermute | solution.py:189
  14.8 0.0 collective-permute-done.3
  14.8 1.6 %collective-permute-start.6 = (bf16[288,128]{1,0:T(8,128)(2,1)S(1)}, bf16[288,128]{1,0:T(8,128)(2,1)S(1)}, u32[]{:S(2)}, u32[]{:S(2)}) collective-permute-start(bf16[288,128]{1,0:T(8,128)(2,1)S(1)} %pad_maximum_fusion.3), channel_id=1, source_target_pairs={{0,2},{1,3},{2,0},{3,1},{4,6},{5,7},{6,4},{7,5},{8,10},{9,11},{10,... | collective-permute-start | bytes 221192 | tf_op jit(solution)/shard_map/ppermute | solution.py:189
  16.4 1.2 %collective-permute-done.4 = bf16[288,128]{1,0:T(8,128)(2,1)S(1)} collective-permute-done((bf16[288,128]{1,0:T(8,128)(2,1)S(1)}, bf16[288,128]{1,0:T(8,128)(2,1)S(1)}, u32[]{:S(2)}, u32[]{:S(2)}) %collective-permute-start.4) | collective-permute-done | bytes 73760 | tf_op jit(solution)/shard_map/ppermute | solution.py:189
  17.6 0.1 collective-permute-start.7
  17.8 0.0 copy-start
  17.8 1.4 %collective-permute-done.6 = bf16[288,128]{1,0:T(8,128)(2,1)S(1)} collective-permute-done((bf16[288,128]{1,0:T(8,128)(2,1)S(1)}, bf16[288,128]{1,0:T(8,128)(2,1)S(1)}, u32[]{:S(2)}, u32[]{:S(2)}) %collective-permute-start.6) | collective-permute-done | bytes 73760 | tf_op jit(solution)/shard_map/ppermute | solution.py:189
  19.2 0.0 collective-permute-done.5
  19.2 0.1 collective-permute-start.8
  19.4 0.2 collective-permute-done.7
  19.6 1.1 %collective-permute-done.8 = bf16[816,128]{1,0:T(8,128)(2,1)S(1)} collective-permute-done((bf16[816,128]{1,0:T(8,128)(2,1)S(1)}, bf16[816,128]{1,0:T(8,128)(2,1)S(1)}, u32[]{:S(2)}, u32[]{:S(2)}) %collective-permute-start.8) | collective-permute-done | bytes 208928 | tf_op jit(solution)/shard_map/ppermute | solution.py:194
  20.8 0.0 copy-done
  20.8 2.2 %shard_map.57 = f32[512,1024]{1,0:T(8,128)} custom-call(s32[8,16]{1,0:T(8,128)S(1)} %bitcast.4, bf16[5504,128]{1,0:T(8,128)(2,1)S(1)} %slice_dynamic-update-slice_fusion.6.blocks, f32[512,1024]{1,0:T(8,128)} %shard_map.56.blank_ref), custom_call_target="tpu_custom_call", output_to_operand_aliasing={{}: (2, {})} | custom-call | tf_op jit(solution)/shard_map/pallas_call | solution.py:167
  (27 shorter events, 0.4 us)
Async XLA Ops:
  0.9 11.6 %collective-permute-start.1 = (bf16[272,128]{1,0:T(8,128)(2,1)S(1)}, bf16[272,128]{1,0:T(8,128)(2,1)S(1)}, u32[]{:S(2)}, u32[]{:S(2)}) collective-permute-start(bf16[272,128]{1,0:T(8,128)(2,1)S(1)} %slice.72), channel_id=1, source_target_pairs={{0,8},{4,12},{8,0},{12,4},{1,9},{5,13},{9,1},{13,5},{2,10},{6,14},... | collective-permute-start | bytes 208904 | tf_op jit(solution)/shard_map/ppermute | solution.py:189
  5.0 7.5 %collective-permute-start.2 = (bf16[272,128]{1,0:T(8,128)(2,1)S(1)}, bf16[272,128]{1,0:T(8,128)(2,1)S(1)}, u32[]{:S(2)}, u32[]{:S(2)}) collective-permute-start(bf16[272,128]{1,0:T(8,128)(2,1)S(1)} %slice.72), channel_id=1, source_target_pairs={{0,4},{4,8},{8,12},{12,0},{1,5},{5,9},{9,13},{13,1},{2,6},{6,10},{... | collective-permute-start | bytes 208904 | tf_op jit(solution)/shard_map/ppermute | solution.py:189
  7.2 5.9 %collective-permute-start = (bf16[416,128]{1,0:T(8,128)(2,1)S(1)}, bf16[416,128]{1,0:T(8,128)(2,1)S(1)}, u32[]{:S(2)}, u32[]{:S(2)}) collective-permute-start(bf16[416,128]{1,0:T(8,128)(2,1)S(1)} %fusion.1), channel_id=1, source_target_pairs={{0,2},{1,3},{2,0},{3,1},{4,6},{5,7},{6,4},{7,5},{8,10},{9,11},{10,... | collective-permute-start | bytes 319496 | tf_op jit(solution)/shard_map/ppermute | solution.py:189
  8.8 5.9 %collective-permute-start.3 = (bf16[272,128]{1,0:T(8,128)(2,1)S(1)}, bf16[272,128]{1,0:T(8,128)(2,1)S(1)}, u32[]{:S(2)}, u32[]{:S(2)}) collective-permute-start(bf16[272,128]{1,0:T(8,128)(2,1)S(1)} %slice.73), channel_id=1, source_target_pairs={{0,12},{4,0},{8,4},{12,8},{1,13},{5,1},{9,5},{13,9},{2,14},{6,2},{... | collective-permute-start | bytes 208904 | tf_op jit(solution)/shard_map/ppermute | solution.py:189
  12.5 6.7 %collective-permute-start.5 = (bf16[544,128]{1,0:T(8,128)(2,1)S(1)}, bf16[544,128]{1,0:T(8,128)(2,1)S(1)}, u32[]{:S(2)}, u32[]{:S(2)}) collective-permute-start(bf16[544,128]{1,0:T(8,128)(2,1)S(1)} %pad_maximum_fusion.1), channel_id=1, source_target_pairs={{0,2},{1,3},{2,0},{3,1},{4,6},{5,7},{6,4},{7,5},{8,10},{9,11},{10,... | collective-permute-start | bytes 417800 | tf_op jit(solution)/shard_map/ppermute | solution.py:189
  13.2 4.4 %collective-permute-start.4 = (bf16[288,128]{1,0:T(8,128)(2,1)S(1)}, bf16[288,128]{1,0:T(8,128)(2,1)S(1)}, u32[]{:S(2)}, u32[]{:S(2)}) collective-permute-start(bf16[288,128]{1,0:T(8,128)(2,1)S(1)} %pad_maximum_fusion.2), channel_id=1, source_target_pairs={{0,16},{16,0},{1,17},{17,1},{2,18},{18,2},{3,19},{19,3},{4,20},{20... | collective-permute-start | bytes 221192 | tf_op jit(solution)/shard_map/ppermute | solution.py:189
  14.8 4.4 %collective-permute-start.6 = (bf16[288,128]{1,0:T(8,128)(2,1)S(1)}, bf16[288,128]{1,0:T(8,128)(2,1)S(1)}, u32[]{:S(2)}, u32[]{:S(2)}) collective-permute-start(bf16[288,128]{1,0:T(8,128)(2,1)S(1)} %pad_maximum_fusion.3), channel_id=1, source_target_pairs={{0,2},{1,3},{2,0},{3,1},{4,6},{5,7},{6,4},{7,5},{8,10},{9,11},{10,... | collective-permute-start | bytes 221192 | tf_op jit(solution)/shard_map/ppermute | solution.py:189
  17.6 1.9 %collective-permute-start.7 = (bf16[1936,128]{1,0:T(8,128)(2,1)S(1)}, bf16[1936,128]{1,0:T(8,128)(2,1)S(1)}, u32[]{:S(2)}, u32[]{:S(2)}) collective-permute-start(bf16[1936,128]{1,0:T(8,128)(2,1)S(1)} %constant_dynamic-update-slice_fusion), channel_id=1, source_target_pairs={{0,1},{1,0},{2,3},{3,2},{4,5},{5,4},{6,7},{7,6},{8,9},{9,8},{10,11... | collective-permute-start | bytes 1486856 | tf_op jit(solution)/shard_map/ppermute | solution.py:194
  17.8 3.1 %copy-start = (s32[16,8]{0,1:T(8,128)S(1)}, s32[16,8]{0,1:T(8,128)}, u32[]{:S(2)}) copy-start(s32[16,8]{0,1:T(8,128)} %param.9) | copy-start | bytes 1540
  19.2 1.5 %collective-permute-start.8 = (bf16[816,128]{1,0:T(8,128)(2,1)S(1)}, bf16[816,128]{1,0:T(8,128)(2,1)S(1)}, u32[]{:S(2)}, u32[]{:S(2)}) collective-permute-start(bf16[816,128]{1,0:T(8,128)(2,1)S(1)} %pad_maximum_fusion), channel_id=1, source_target_pairs={{0,1},{1,0},{2,3},{3,2},{4,5},{5,4},{6,7},{7,6},{8,9},{9,8},{10,11... | collective-permute-start | bytes 626696 | tf_op jit(solution)/shard_map/ppermute | solution.py:194
